TPU v7x, 512 devices: a whole 4x8x8 slice. The times are simulated.
512 devices in a mesh: dp: 2 (over core), ctx: 32 (over x, y), exp: 8 (over z).
Axes of the slice: x: 4, y: 8, z: 8, core: 2. Of those that a mesh axis runs over, the one named last changes fastest.
Arguments:
- residual: bfloat16 [2, 4096, 2048], P('dp', 'ctx'), may hold values from -6 to 6
- queries: bfloat16 [2, 4096, 2, 1024], P('dp', 'ctx', None, 'exp'), may hold values from -20 to 20
- keys: bfloat16 [2, 4096, 1024], P('dp', 'ctx', 'exp'), may hold values from -20 to 20
- values: bfloat16 [2, 4096, 1024], P('dp', 'ctx', 'exp'), may hold values from -6 to 6
- attn_routes: int32 [2, 4096, 2], P('dp', 'ctx'), may hold values from 0 to 7, all different within a row; in each aligned block of 128 rows (0 to 127, 128 to 255, ..., all dimensions but the last counted through in order) at most 40 rows name the same one
- attn_gates: float32 [2, 4096, 2], P('dp', 'ctx'), may hold values from 0.3 to 1
- out_weight: bfloat16 [8, 1024, 2048], P('exp', None, 'ctx'), may hold values from -0.75 to 0.75
- norm_gain: float32 [2048], replicated, may hold values from 0.5 to 1.5
- ffn_routes: int32 [2, 4096, 2], P('dp', 'ctx'), may hold values from 0 to 7, all different within a row; in each aligned block of 128 rows (0 to 127, 128 to 255, ..., all dimensions but the last counted through in order) at most 32 rows name the same one
- ffn_gates: float32 [2, 4096, 2], P('dp', 'ctx'), may hold values from 0.3 to 1
- w_gate: bfloat16 [8, 2048, 5632], P('exp', None, 'ctx'), may hold values from -0.125 to 0.125
- w_up: bfloat16 [8, 2048, 5632], P('exp', None, 'ctx'), may hold values from -0.125 to 0.125
- w_down: bfloat16 [8, 5632, 2048], P('exp', 'ctx'), may hold values from -0.15625 to 0.15625
Outputs:
- layer_out: bfloat16 [2, 4096, 2048], P('dp', 'ctx')
Inputs may be any that keep to these rules, and one draw needn't show every extreme that they name: `attn_routes`: no attention expert is named by more than 40 of the rows of one device; a row's two experts differ. `ffn_routes`: every FFN expert is named by exactly 32 of the rows of one device; a row's two experts differ.
All inputs are finite; a program needn't handle non-finite values.
Results may differ from a plain program's by a relative error of at most 0.02.
Values may be sent and summed in bfloat16 or wider, within the bound.
A program may use at most 64 MiB of HBM per device.

v0:
```python
import math

import jax
import jax.numpy as jnp
from jax import lax
from jax.sharding import PartitionSpec as P

HEAD = 128


NEG_FILL = -1e30


def rms_norm(stream_rows, gain_vector):
    mean_square = jnp.mean(stream_rows * stream_rows, axis=-1, keepdims=True)
    return (stream_rows * lax.rsqrt(mean_square + 1e-06) * gain_vector).astype(jnp.bfloat16)


def slot_ranks(routes_flat, experts):
    onehot = (routes_flat[:, None] == jnp.arange(experts, dtype=jnp.int32)[None, :]).astype(
        jnp.int32
    )
    before = jnp.cumsum(onehot, axis=0) - onehot
    return jnp.sum(before * onehot, axis=1)


def shards(
    residual,
    queries,
    keys,
    values,
    attn_routes,
    attn_gates,
    out_weight,
    norm_gain,
    ffn_routes,
    ffn_gates,
    w_gate,
    w_up,
    w_down,
):
    tok_dev = residual.shape[1]
    width = residual.shape[2]
    local_heads = keys.shape[2] // HEAD
    experts = lax.axis_size("exp")
    my_expert = lax.axis_index("exp")
    first_pos = lax.axis_index("ctx") * tok_dev
    slot_rows = tok_dev * 2
    score_scale = 1.0 / math.sqrt(HEAD)
    query_rows = queries.reshape(slot_rows, local_heads, HEAD)
    query_pos = first_pos + jnp.arange(slot_rows, dtype=jnp.int32) // 2
    run_max = jnp.full((local_heads, slot_rows), NEG_FILL, jnp.float32)
    key_piece = lax.all_gather(keys, "ctx", axis=1, tiled=True).reshape(-1, local_heads, HEAD)
    value_piece = lax.all_gather(values, "ctx", axis=1, tiled=True).reshape(-1, local_heads, HEAD)
    key_count = key_piece.shape[0]
    scores = (
        jnp.einsum("qhd,khd->hqk", query_rows, key_piece, preferred_element_type=jnp.float32)
        * score_scale
    )
    key_pos = jnp.arange(key_count, dtype=jnp.int32)
    allowed = (key_pos[None, :] <= query_pos[:, None])[None]
    masked = jnp.where(allowed, scores, NEG_FILL)
    new_max = jnp.maximum(run_max, jnp.max(masked, axis=2))
    weights = jnp.where(allowed, jnp.exp(scores - new_max[:, :, None]), 0.0)
    new_total = jnp.sum(weights, axis=2)
    update = jnp.einsum(
        "hqk,khd->hqd",
        weights.astype(jnp.bfloat16),
        value_piece,
        preferred_element_type=jnp.float32,
    )
    attended = (update / new_total[:, :, None]).astype(jnp.bfloat16)
    attended = jnp.transpose(attended, (1, 0, 2)).reshape(slot_rows, local_heads * HEAD)
    attn_cap = min(tok_dev, 5 * tok_dev // (2 * experts))
    attn_flat = attn_routes.reshape(slot_rows)
    attn_rank = slot_ranks(attn_flat, experts)
    attn_slot = attn_flat * attn_cap + attn_rank
    dispatch = (
        jnp.arange(experts * attn_cap, dtype=jnp.int32)[:, None] == attn_slot[None, :]
    ).astype(jnp.bfloat16)
    packed = jnp.dot(dispatch, attended, preferred_element_type=jnp.float32).astype(jnp.bfloat16)
    packed = packed.reshape(experts, attn_cap, local_heads * HEAD)
    expert_rows = lax.all_to_all(packed, "exp", split_axis=0, concat_axis=2, tiled=True)[0]
    projected = jnp.dot(
        expert_rows,
        lax.all_gather(out_weight, "ctx", axis=2, tiled=True)[0],
        preferred_element_type=jnp.float32,
    ).astype(jnp.bfloat16)
    picked = jnp.take(projected, attn_rank, axis=0).astype(jnp.float32)
    attn_weight = jnp.where(attn_flat == my_expert, attn_gates.reshape(slot_rows), 0.0)
    attn_part = jnp.sum((picked * attn_weight[:, None]).reshape(tok_dev, 2, width), axis=1)
    ffn_cap = 2 * tok_dev // experts
    ffn_flat = ffn_routes.reshape(slot_rows)
    ffn_rank = slot_ranks(ffn_flat, experts)
    ffn_slot = ffn_flat * ffn_cap + ffn_rank
    token_of = jnp.arange(slot_rows, dtype=jnp.int32) // 2
    slot_token = jnp.zeros((experts * ffn_cap,), jnp.int32).at[ffn_slot].set(token_of)
    own_tokens = lax.dynamic_slice_in_dim(slot_token, my_expert * ffn_cap, ffn_cap)
    residual_rows = residual[0].astype(jnp.float32)
    attn_out = lax.psum(attn_part.astype(jnp.bfloat16), "exp").astype(jnp.float32)
    resid = residual_rows + attn_out
    normed = rms_norm(resid, norm_gain)
    ffn_in = jnp.take(normed, own_tokens, axis=0)
    shard_rows = lax.all_gather(ffn_in, "ctx", axis=0, tiled=True)
    gate_proj = jnp.dot(shard_rows, w_gate[0], preferred_element_type=jnp.float32)
    up_proj = jnp.dot(shard_rows, w_up[0], preferred_element_type=jnp.float32)
    hidden = (jax.nn.silu(gate_proj) * up_proj).astype(jnp.bfloat16)
    partial_sums = jnp.dot(hidden, w_down[0], preferred_element_type=jnp.float32)
    ffn_rows = lax.psum_scatter(
        partial_sums.astype(jnp.bfloat16), "ctx", scatter_dimension=0, tiled=True
    ).astype(jnp.float32)
    ffn_picked = jnp.take(ffn_rows, ffn_rank, axis=0)
    ffn_weight = jnp.where(ffn_flat == my_expert, ffn_gates.reshape(slot_rows), 0.0)
    ffn_part = jnp.sum((ffn_picked * ffn_weight[:, None]).reshape(tok_dev, 2, width), axis=1)
    layer_total = lax.psum(ffn_part.astype(jnp.bfloat16), "exp").astype(jnp.float32)
    return (resid + layer_total).astype(jnp.bfloat16)[None]


def solution(mesh):
    in_specs = (
        P("dp", "ctx", None),
        P("dp", "ctx", None, "exp"),
        P("dp", "ctx", "exp"),
        P("dp", "ctx", "exp"),
        P("dp", "ctx", None),
        P("dp", "ctx", None),
        P("exp", None, "ctx"),
        P(),
        P("dp", "ctx", None),
        P("dp", "ctx", None),
        P("exp", None, "ctx"),
        P("exp", None, "ctx"),
        P("exp", "ctx", None),
    )
    out_specs = P("dp", "ctx", None)
    return jax.shard_map(shards, mesh=mesh, in_specs=in_specs, out_specs=out_specs, check_vma=False)
```

profile of v0, /device:TPU:6, one launch (start us, length us, event | category | flops | bytes accessed | tf_op | source)
XLA Modules:
  0.0 777.7 jit_solution(13068956776990536037)
XLA Ops:
  14.1 81.4 %all-gather.5.cloned.1.call-done = bf16[1,4096,128]{2,1,0:T(8,128)(2,1)} async-done(((bf16[1,128,128]{2,1,0:T(8,128)(2,1)}), bf16[1,4096,128]{2,1,0:T(8,128)(2,1)}) %all-gather.5.cloned.1.call-update) | async-done | bytes 1048592 | tf_op jit(solution)/shard_map/all_gather | solution.py:53
  95.4 2.3 select_reduce_fusion
  97.7 2.0 copy-done.3
  100.8 77.3 %all-gather.7.cloned.1.call-done = bf16[1,4096,128]{2,1,0:T(8,128)(2,1)} async-done(((bf16[1,128,128]{2,1,0:T(8,128)(2,1)}), bf16[1,4096,128]{2,1,0:T(8,128)(2,1)}) %all-gather.7.cloned.1.call-update) | async-done | bytes 1048592 | tf_op jit(solution)/shard_map/all_gather | solution.py:54
  178.0 4.4 convolution_convert_fusion.1
  182.4 7.4 all-to-all-start
  190.5 7.9 %all-to-all-done = bf16[8,40,128]{2,1,0:T(8,128)(2,1)S(1)} async-done(((bf16[8,40,128]{2,1,0:T(8,128)(2,1)}), bf16[8,40,128]{2,1,0:T(8,128)(2,1)S(1)}, u32[]{:S(2)}, u32[]{:S(2)}) %all-to-all-start) | async-done | bytes 81952 | tf_op jit(solution)/shard_map/all_to_all | solution.py:83
  198.4 67.1 %all-gather.9.cloned.1.call-done = bf16[1,1024,2048]{1,2,0:T(8,128)(2,1)} async-done(((bf16[1,1024,64]{1,2,0:T(8,128)(2,1)}), bf16[1,1024,2048]{1,2,0:T(8,128)(2,1)}) %all-gather.9.cloned.1.call-update) | async-done | bytes 4194320 | tf_op jit(solution)/shard_map/all_gather | solution.py:86
  265.4 3.5 fusion.4
  269.0 1.4 gather_fusion
  271.1 4.9 multiply_reduce_fusion.1
  276.1 1.4 scatter_custom_fusion
  277.6 77.8 %all-reduce.3.cloned.1.call-done = bf16[128,2048]{1,0:T(8,128)(2,1)} async-done(((bf16[128,2048]{1,0:T(8,128)(2,1)}), bf16[128,2048]{1,0:T(8,128)(2,1)}) %all-reduce.3.cloned.1.call-update) | async-done | bytes 524304 | tf_op jit(solution)/shard_map/psum | solution.py:100
  355.4 1.3 multiply_reduce_fusion.2
  356.7 1.3 multiply_convert_fusion
  359.7 82.9 %all-gather.11.cloned.1.call-done = bf16[1024,2048]{1,0:T(8,128)(2,1)} async-done(((bf16[32,2048]{1,0:T(8,128)(2,1)}), bf16[1024,2048]{1,0:T(8,128)(2,1)}) %all-gather.11.cloned.1.call-update) | async-done | bytes 4194320 | tf_op jit(solution)/shard_map/all_gather | solution.py:104
  442.6 3.7 fusion.24
  446.4 6.9 convolution_convert_fusion
  454.1 224.0 %reduce-scatter.2.cloned.1.call-done = bf16[32,2048]{1,0:T(8,128)(2,1)} async-done(((bf16[1024,2048]{1,0:T(8,128)(2,1)}), bf16[32,2048]{1,0:T(8,128)(2,1)}) %reduce-scatter.2.cloned.1.call-update) | async-done | bytes 131088 | tf_op jit(solution)/shard_map/reduce_scatter | solution.py:109
  679.0 1.5 gather_fusion.2
  680.5 2.3 gather.20
  682.8 6.4 multiply_reduce_fusion
  689.2 79.5 %all-reduce.5.cloned.1.call-done = bf16[128,2048]{1,0:T(8,128)(2,1)} async-done(((bf16[128,2048]{1,0:T(8,128)(2,1)}), bf16[128,2048]{1,0:T(8,128)(2,1)}) %all-reduce.5.cloned.1.call-update) | async-done | bytes 524304 | tf_op jit(solution)/shard_map/psum | solution.py:115
  768.7 2.2 fusion.31
  (76 shorter events, 13.5 us)
Async XLA Ops:
  6.5 439.8 %copy-start = (bf16[1,176,2048]{2,1,0:T(8,128)(2,1)S(1)}, bf16[1,176,2048]{2,1,0:T(8,128)(2,1)}, u32[]{:S(2)}) copy-start(bf16[1,176,2048]{2,1,0:T(8,128)(2,1)} %param.25) | copy-start | bytes 2162692
  6.5 88.9 %all-gather.5.cloned.1.call-start = ((), (), s32[]{:S(2)}) async-start(), calls=%async_computation.2 | async-start | bytes 1081344 | tf_op jit(solution)/shard_map/all_gather | solution.py:53
  7.3 170.8 %all-gather.7.cloned.1.call-start = ((), (), s32[]{:S(2)}) async-start(), calls=%async_computation.3 | async-start | bytes 1081344 | tf_op jit(solution)/shard_map/all_gather | solution.py:54
  8.0 257.4 %all-gather.9.cloned.1.call-start = ((), (), s32[]{:S(2)}) async-start(), calls=%async_computation.4 | async-start | bytes 4325376 | tf_op jit(solution)/shard_map/all_gather | solution.py:86
  97.7 2.0 copy-start.3
  182.4 15.9 %all-to-all-start = ((bf16[8,40,128]{2,1,0:T(8,128)(2,1)}), bf16[8,40,128]{2,1,0:T(8,128)(2,1)S(1)}, u32[]{:S(2)}, u32[]{:S(2)}) async-start(bf16[8,40,128]{2,1,0:T(8,128)(2,1)} %bitcast.6), calls=%async_computation | async-start | bytes 163840 | tf_op jit(solution)/shard_map/all_to_all | solution.py:83
  189.8 165.6 %all-reduce.3.cloned.1.call-start = ((), (), s32[]{:S(2)}) async-start(), calls=%async_computation.5 | async-start | bytes 1048576 | tf_op jit(solution)/shard_map/psum | solution.py:100
  270.4 85.0 %copy-start.1 = (bf16[1,128,2048]{2,1,0:T(8,128)(2,1)S(1)}, bf16[1,128,2048]{2,1,0:T(8,128)(2,1)}, u32[]{:S(2)}) copy-start(bf16[1,128,2048]{2,1,0:T(8,128)(2,1)} %param.13) | copy-start | bytes 1572868
  270.4 86.3 %copy-start.5 = (f32[2048]{0:T(1024)S(1)}, f32[2048]{0:T(1024)}, u32[]{:S(2)}) copy-start(f32[2048]{0:T(1024)} %param.20) | copy-start | bytes 24580
  276.0 166.6 %copy-start.7 = (bf16[1,2048,176]{1,2,0:T(8,128)(2,1)S(1)}, bf16[1,2048,176]{1,2,0:T(8,128)(2,1)}, u32[]{:S(2)}) copy-start(bf16[1,2048,176]{1,2,0:T(8,128)(2,1)} %param.23) | copy-start | bytes 2162692
  276.0 166.6 %all-gather.11.cloned.1.call-start = ((), (), s32[]{:S(2)}) async-start(), calls=%async_computation.6 | async-start | bytes 4325376 | tf_op jit(solution)/shard_map/all_gather | solution.py:104
  356.7 89.7 %copy-start.8 = (bf16[1,2048,176]{1,2,0:T(8,128)(2,1)S(1)}, bf16[1,2048,176]{1,2,0:T(8,128)(2,1)}, u32[]{:S(2)}) copy-start(bf16[1,2048,176]{1,2,0:T(8,128)(2,1)} %param.24) | copy-start | bytes 2162692
  359.5 318.6 %reduce-scatter.2.cloned.1.call-start = ((), (), s32[]{:S(2)}) async-start(), calls=%async_computation.7 | async-start | bytes 4325376 | tf_op jit(solution)/shard_map/reduce_scatter | solution.py:109
  453.2 0.7 copy-start.4
  453.2 0.7 copy-start.6
  453.3 315.4 %all-reduce.5.cloned.1.call-start = ((), (), s32[]{:S(2)}) async-start(), calls=%async_computation.8 | async-start | bytes 1048576 | tf_op jit(solution)/shard_map/psum | solution.py:115
  680.4 88.2 %copy-start.2 = (bf16[1,128,2048]{2,1,0:T(8,128)(2,1)S(1)}, bf16[1,128,2048]{2,1,0:T(8,128)(2,1)}, u32[]{:S(2)}) copy-start(bf16[1,128,2048]{2,1,0:T(8,128)(2,1)} %param.13) | copy-start | bytes 1572868
Sparse Core Ops, SparseCore 0:
  10.5 84.8 all-gather.4
  98.6 79.3 all-gather.6
  181.2 84.1 all-gather.8
  276.2 79.1 all-reduce.2
  359.6 82.9 all-gather.10
  453.4 224.6 reduce-scatter.1
  689.3 79.3 all-reduce.4
where the time goes:
time: 778 us
  waiting for transfers between devices  700 us (90%)
  other arithmetic  21.9 us (3%)
  matrix products  20.8 us (3%)
  local copies, waits for them, and re-layouts  13.7 us (2%)
  between operations  13.7 us (2%)
  starting transfers between devices  7.8 us (1%)
    reduce_scatter x1, waiting for transfers between devices, shards(): lax.psum_scatter(partial_sums.astype(jnp.bfloat16), 'ctx', scatter_dimens...  224 us
    all_gather x1, waiting for transfers between devices, shards(): shard_rows = lax.all_gather(ffn_in, 'ctx', axis=0, tiled=True)  82.9 us
    all_gather x1, waiting for transfers between devices, shards(): lax.all_gather(keys, 'ctx', axis=1, tiled=True)  81.4 us
    psum x1, waiting for transfers between devices, shards(): lax.psum(ffn_part.astype(jnp.bfloat16), 'exp').astype(jnp.float32)  79.5 us
    psum x1, waiting for transfers between devices, shards(): lax.psum(attn_part.astype(jnp.bfloat16), 'exp').astype(jnp.float32)  77.8 us
    all_gather x1, waiting for transfers between devices, shards(): lax.all_gather(values, 'ctx', axis=1, tiled=True)  77.3 us
    all_gather x1, waiting for transfers between devices, shards(): lax.all_gather(out_weight, 'ctx', axis=2, tiled=True)[0]  67.1 us
  transfers between devices with their start and end apart: 8, of which 8 were waited for; matrix products, arithmetic and copies ran while one was open for 2% of the time, Pallas kernels for 0%

commit v1 on v0

v1 whole, which is shorter than its diff:
```python
import functools
import math

import jax
import jax.numpy as jnp
from jax import lax
from jax.experimental import pallas as pl
from jax.experimental.pallas import tpu as pltpu
from jax.sharding import PartitionSpec as P

MESH = pl.DeviceIdType.MESH
BF = jnp.bfloat16
F32 = jnp.float32
NX, NY, NZ = 4, 8, 8
TOK = 128
D = 2048
HEAD = 128
ACAP = 48
FCAP = 32
NEG = -1e30


def nt(a, b):
    return lax.dot_general(a, b, (((1,), (1,)), ((), ())), preferred_element_type=F32)


def tn(a, b):
    return lax.dot_general(a, b, (((0,), (0,)), ((), ())), preferred_element_type=F32)


def nn(a, b):
    return jnp.dot(a, b, preferred_element_type=F32)


def wrap(v, n):
    return lax.rem(v + 2 * n, n)


class Copies:
    def __init__(self):
        self.sent = []

    def send(self, src, dst, ssem, rsem, dev):
        cp = pltpu.make_async_remote_copy(
            src_ref=src, dst_ref=dst, send_sem=ssem, recv_sem=rsem, device_id=dev, device_id_type=MESH
        )
        cp.start()
        self.sent.append(cp)
        return cp

    def drain(self):
        for cp in self.sent:
            cp.wait_send()


class Ring:
    def __init__(self, copies, at, pos, right, left, ssem, rsem, chunks):
        self.copies, self.at, self.pos = copies, at, pos
        self.devs = (right, left)
        self.ssem, self.rsem, self.chunks = ssem, rsem, chunks
        self.cps = {}

    def carries(self, way, step, j):
        return step < 4 or (j < self.chunks // 2) == (way == 0)

    def slot(self, way, step):
        return wrap(self.pos - step if way == 0 else self.pos + step, 8)

    def start(self, step, j, own=None):
        for way in (0, 1):
            if self.carries(way, step, j):
                slot = self.slot(way, step - 1)
                src = self.at(slot, j) if own is None else own(j)
                self.cps[way, step, j] = self.copies.send(
                    src, self.at(slot, j), self.ssem.at[way, step - 1, j], self.rsem.at[way, step - 1, j], self.devs[way]
                )

    def wait(self, step, j):
        for way in (0, 1):
            if self.carries(way, step, j):
                self.cps[way, step, j].wait_recv()

    def forward(self, step, own=None):
        for j in range(self.chunks):
            if step > 1:
                self.wait(step - 1, j)
            self.start(step, j, own if step == 1 else None)

    def finish(self):
        for j in range(self.chunks):
            self.wait(4, j)


def layer_kernel(
    meta, res, q, kv, gain, wo, gu, wd, out,
    KV, QB, OB, SB, OS, SS, WO, GU, WD, PK, ER, PR, MG, FG, XN, YP, RR, RL, EO, RES,
    bsem, kv_s, kv_r, q_s, q_r, o_s, o_r, wx_s, wx_r, wy_s, wy_r, wc_s, wc_r,
    fx_s, fx_r, fc_s, fc_r, a_s, a_r, p_s, p_r, x_s, x_r, y_s, y_r, e_s, e_r,
):
    j = lax.axis_index("dp")
    c = lax.axis_index("ctx")
    z = lax.axis_index("exp")
    x = c // NY
    y = c % NY
    cop = Copies()

    def xdev(k):
        return (j, wrap(x + k, NX) * NY + y, z)

    def ydev(k):
        return (j, x * NY + wrap(y + k, NY), z)

    def zdev(k):
        return (j, c, wrap(z + k, NZ))

    sib = (1 - j, c, z)
    half = lambda n, i: pl.ds(pl.multiple_of(i * n, n), n)

    for d in range(1, NX):
        OB[d] = jnp.zeros((HEAD, 2 * TOK), BF)
        SB[d] = jnp.concatenate(
            [jnp.full((1, 2 * TOK), NEG, F32), jnp.zeros((7, 2 * TOK), F32)], axis=0
        )

    barrier = pltpu.get_barrier_semaphore()
    partners = [xdev(k) for k in (1, 2, 3)] + [ydev(1), ydev(-1)] + [zdev(k) for k in range(1, 8)] + [sib]
    for dev in partners:
        pl.semaphore_signal(barrier, inc=1, device_id=dev, device_id_type=MESH)
    pl.semaphore_wait(barrier, len(partners))

    kvring = Ring(
        cop, lambda slot, k: KV.at[slot, k], y, ydev(1), ydev(-1), kv_s, kv_r, 2
    )
    kvring.forward(1, own=lambda k: kv.at[k])

    for d in range(1, NX):

        @pl.when(x >= d)
        def _():
            pltpu.make_async_remote_copy(
                src_ref=q, dst_ref=QB.at[d], send_sem=q_s.at[d], recv_sem=q_r.at[d],
                device_id=xdev(-d), device_id_type=MESH,
            ).start()

    own_w = [
        pltpu.make_async_copy(wo.at[half(256, j)], WO.at[x, y, half(256, j)], bsem.at[0]),
        pltpu.make_async_copy(gu, GU.at[x], bsem.at[1]),
        pltpu.make_async_copy(wd, WD.at[x], bsem.at[2]),
    ]
    for cp in own_w:
        cp.start()
    wx = [
        cop.send(
            wo.at[half(256, j)], WO.at[x, y, half(256, j)], wx_s.at[d - 1], wx_r.at[d - 1], xdev(d)
        )
        for d in (1, 2, 3)
    ]

    grow = half(1024, j)
    fx = []
    for way, step in ((0, 1), (1, -1)):
        fx.append(cop.send(gu.at[grow], GU.at[x, grow], fx_s.at[way, 0], fx_r.at[way, 0], xdev(step)))
        fx.append(
            cop.send(wd.at[:, grow], WD.at[x, :, grow], fx_s.at[way, 1], fx_r.at[way, 1], xdev(step))
        )

    KV[y] = kv[...]

    ar = jnp.concatenate([meta[0:1, :], meta[1:2, :]], axis=1)
    fr = jnp.concatenate([meta[4:5, :], meta[5:6, :]], axis=1)
    upper = (
        lax.broadcasted_iota(jnp.int32, (256, 256), 0) < lax.broadcasted_iota(jnp.int32, (256, 256), 1)
    ).astype(F32).astype(BF)

    def slots(route, cap):
        eid = lax.broadcasted_iota(jnp.int32, (8, 256), 0).astype(F32)
        onehot = (eid == route).astype(F32)
        before = nn(onehot.astype(BF), upper)
        return route * cap + jnp.sum(before * onehot, axis=0, keepdims=True)

    def iota0(rows, cols):
        return lax.broadcasted_iota(jnp.int32, (rows, cols), 0).astype(F32)

    aslot = slots(ar, ACAP)
    fslot = slots(fr, FCAP)
    disp = (iota0(8 * ACAP, 256) == aslot).astype(F32).astype(BF)

    def gate_table(slot, g0, g1, rows):
        rid = iota0(rows, TOK)
        t = jnp.where(rid == slot[:, :TOK], g0, 0.0) + jnp.where(rid == slot[:, TOK:], g1, 0.0)
        t = t.T
        hi = t.astype(BF)
        return hi, (t - hi.astype(F32)).astype(BF)

    mhi, mlo = gate_table(aslot, meta[2:3, :], meta[3:4, :], 8 * ACAP)
    MG[0] = mhi
    MG[1] = mlo
    fhi, flo = gate_table(fslot, meta[6:7, :], meta[7:8, :], 8 * FCAP)
    FG[0] = fhi
    FG[1] = flo
    mine = iota0(FCAP, TOK) + (z * FCAP).astype(F32)
    sel = (
        (mine == fslot[:, :TOK]).astype(F32) + (mine == fslot[:, TOK:]).astype(F32)
    ).astype(BF)

    kvring.forward(2)

    for cp in wx:
        cp.wait_recv()
    own_w[0].wait()
    wring = Ring(
        cop,
        lambda slot, k: WO.at[pl.ds(2 * k, 2), slot, half(256, j)],
        y, ydev(1), ydev(-1), wy_s, wy_r, 2,
    )
    wcs = []

    def to_sibling(n, slot):
        wcs.append(
            cop.send(
                WO.at[:, slot, half(256, j)], WO.at[:, slot, half(256, j)], wc_s.at[n], wc_r.at[n], sib
            )
        )

    kvring.forward(3)
    wring.forward(1)
    to_sibling(0, y)
    kvring.forward(4)
    kvring.finish()

    scale = 1.0 / math.sqrt(HEAD)
    keys = KV[:, 0].reshape(NY * TOK, HEAD)
    vals = KV[:, 1].reshape(NY * TOK, HEAD)

    def attend(queries, masked):
        s = nt(keys, queries) * scale
        if masked:
            kpos = lax.broadcasted_iota(jnp.int32, (NY * TOK, 2 * TOK), 0)
            lane = lax.broadcasted_iota(jnp.int32, (NY * TOK, 2 * TOK), 1)
            qpos = y * TOK + jnp.bitwise_and(lane, TOK - 1)
            s = jnp.where(kpos <= qpos, s, NEG)
        m = jnp.max(s, axis=0, keepdims=True)
        p = jnp.exp(s - m)
        l = jnp.sum(p, axis=0, keepdims=True)
        return tn(vals, p.astype(BF)), m, l

    for d in range(1, NX):

        @pl.when(x + d < NX)
        def _():
            pltpu.make_async_remote_copy(
                src_ref=q, dst_ref=QB.at[d], send_sem=q_s.at[d], recv_sem=q_r.at[d],
                device_id=xdev(-d), device_id_type=MESH,
            ).wait_recv()
            o, m, l = attend(QB[d], False)
            OS[d] = o.astype(BF)
            SS[d] = jnp.concatenate([m, l, jnp.zeros((6, 2 * TOK), F32)], axis=0)
            for src, dst, i in ((OS, OB, 0), (SS, SB, 1)):
                pltpu.make_async_remote_copy(
                    src_ref=src.at[d], dst_ref=dst.at[d], send_sem=o_s.at[d, i], recv_sem=o_r.at[d, i],
                    device_id=xdev(d), device_id_type=MESH,
                ).start()

    o, m, l = attend(q[...], True)

    wring.forward(2)
    to_sibling(1, wrap(y - 1, NY))
    to_sibling(2, wrap(y + 1, NY))

    for d in range(1, NX):

        @pl.when(x >= d)
        def _():
            for src, dst, i in ((OS, OB, 0), (SS, SB, 1)):
                pltpu.make_async_remote_copy(
                    src_ref=src.at[d], dst_ref=dst.at[d], send_sem=o_s.at[d, i], recv_sem=o_r.at[d, i],
                    device_id=xdev(d), device_id_type=MESH,
                ).wait_recv()

    top = m
    for d in range(1, NX):
        top = jnp.maximum(top, SB[d, 0:1, :])
    f = jnp.exp(m - top)
    o = o * f
    l = l * f
    for d in range(1, NX):
        f = jnp.exp(SB[d, 0:1, :] - top)
        o = o + OB[d].astype(F32) * f
        l = l + SB[d, 1:2, :] * f
    attended = (o / l).astype(BF)

    packed = nt(disp, attended).astype(BF)
    PK[...] = packed.reshape(NZ, ACAP, HEAD)
    acps = []
    for k in range(1, NZ):
        acps.append(
            cop.send(PK.at[wrap(z + k, NZ)], ER.at[z], a_s.at[k], a_r.at[k], zdev(k))
        )
    ER[z] = PK[z]

    wring.forward(3)
    to_sibling(3, wrap(y - 2, NY))
    to_sibling(4, wrap(y + 2, NY))

    for cp in fx:
        cp.wait_recv()
    ahead = []
    for way, step, base in ((0, 1, 0), (1, -1, 512)):
        rows = pl.ds(pl.multiple_of(j * 1024 + base, 512), 512)
        slot = wrap(x - step, NX)
        ahead.append(
            cop.send(GU.at[slot, rows], GU.at[slot, rows], fx_s.at[way, 2], fx_r.at[way, 2], xdev(step))
        )
        ahead.append(
            cop.send(
                WD.at[slot, :, rows], WD.at[slot, :, rows], fx_s.at[way, 3], fx_r.at[way, 3], xdev(step)
            )
        )
    fcs = []

    def weights_to_sibling(n, slot):
        fcs.append(cop.send(GU.at[slot, grow], GU.at[slot, grow], fc_s.at[n, 0], fc_r.at[n, 0], sib))
        fcs.append(
            cop.send(WD.at[slot, :, grow], WD.at[slot, :, grow], fc_s.at[n, 1], fc_r.at[n, 1], sib)
        )

    weights_to_sibling(0, wrap(x - 1, NX))
    weights_to_sibling(1, wrap(x + 1, NX))

    wring.forward(4)
    to_sibling(5, wrap(y - 3, NY))
    to_sibling(6, wrap(y + 3, NY))
    wring.finish()
    to_sibling(7, wrap(y + 4, NY))

    for cp in acps:
        cp.wait_recv()
    lhs = jnp.concatenate(
        [
            jnp.concatenate([ER[h] for h in range(4)], axis=1),
            jnp.concatenate([ER[h] for h in range(4, 8)], axis=1),
        ],
        axis=0,
    )
    for cp in wcs:
        cp.wait_recv()
    low = lax.broadcasted_iota(jnp.int32, (ACAP, HEAD), 1) < 64
    for i in range(NX * NY // 2):
        a, b = 2 * i, 2 * i + 1
        w = jnp.concatenate([WO[a // NY, a % NY], WO[b // NY, b % NY]], axis=1)
        r = nn(lhs, w)
        ra0, ra1 = r[:ACAP, :HEAD], r[ACAP:, :HEAD]
        rb0, rb1 = r[:ACAP, HEAD:], r[ACAP:, HEAD:]
        first = ra0 + pltpu.roll(ra1, 64, 1)
        second = pltpu.roll(rb0, 64, 1) + rb1
        PR[z, :, i * HEAD:(i + 1) * HEAD] = jnp.where(low, first, second).astype(BF)

    pring = Ring(
        cop, lambda slot, k: PR.at[slot, :, k * 512:(k + 1) * 512], z, zdev(1), zdev(-1), p_s, p_r, 4
    )
    for step in (1, 2, 3, 4):
        pring.forward(step)
    pring.finish()

    rows_all = PR[...].reshape(NZ * ACAP, D)
    own_hi = nn(sel, MG[0]).astype(BF)
    own_lo = nn(sel, MG[1]).astype(BF)
    own = nn(sel, res[...]) + nn(own_hi, rows_all) + nn(own_lo, rows_all)
    ms = jnp.mean(own * own, axis=1, keepdims=True)
    XN[y] = (own * lax.rsqrt(ms + 1e-6) * gain[...]).astype(BF)

    xring = Ring(
        cop, lambda slot, k: XN.at[slot, :, k * 512:(k + 1) * 512], y, ydev(1), ydev(-1), x_s, x_r, 4
    )
    xring.forward(1)
    RES[...] = res[...].astype(F32) + nn(MG[0], rows_all) + nn(MG[1], rows_all)
    xring.forward(2)
    for cp in ahead:
        cp.wait_recv()
    weights_to_sibling(2, wrap(x + 2, NX))
    xring.forward(3)
    xring.forward(4)
    xring.finish()
    own_w[1].wait()
    own_w[2].wait()
    for cp in fcs:
        cp.wait_recv()

    rows = XN[...].reshape(NY * FCAP, D)
    wide = []
    tails = []
    for i in range(2):
        a, b = 2 * i, 2 * i + 1
        g = nn(rows, jnp.concatenate([GU[a, :, 0:128], GU[b, :, 0:128]], axis=1))
        u = nn(rows, jnp.concatenate([GU[a, :, 256:384], GU[b, :, 256:384]], axis=1))
        t = nn(rows, jnp.concatenate([GU[a, :, 128:256], GU[b, :, 128:256]], axis=1))
        wide.append((g / (1.0 + jnp.exp(-g)) * u).astype(BF))
        for k in range(2):
            tk = t[:, k * 128:(k + 1) * 128]
            tails.append(tk / (1.0 + jnp.exp(-tk)) * pltpu.roll(tk, 64, 1))
    lowr = lax.broadcasted_iota(jnp.int32, (NY * FCAP, HEAD), 1) < 64
    tail = jnp.concatenate(
        [
            jnp.where(lowr, tails[0], pltpu.roll(tails[1], 64, 1)),
            jnp.where(lowr, tails[2], pltpu.roll(tails[3], 64, 1)),
        ],
        axis=1,
    ).astype(BF)
    hidden = jnp.concatenate([wide[0], wide[1], tail], axis=1)
    pad = jnp.zeros((16, 512), BF)
    for n in range(4):
        cols = slice(n * 512, (n + 1) * 512)
        w = jnp.concatenate(
            [WD[k, 0:128, cols] for k in range(4)]
            + [v for k in range(4) for v in (WD[k, 128:176, cols], pad)],
            axis=0,
        )
        YP[:, :, cols] = nn(hidden, w).astype(BF).reshape(NY, FCAP, 512)

    rcp, lcp = {}, {}
    for step in (1, 2, 3, 4):
        rd, ld = wrap(y + 5 - step, NY), wrap(y - 5 + step, NY)
        if step == 2:
            rcp[1].wait_recv()
            YP[rd, :, 0:1024] = (YP[rd, :, 0:1024].astype(F32) + RR[0, :, 0:1024].astype(F32)).astype(BF)
            lcp[1].wait_recv()
            YP[ld, :, 1024:2048] = (
                YP[ld, :, 1024:2048].astype(F32) + RL[0, :, 1024:2048].astype(F32)
            ).astype(BF)
        elif step > 2:
            rcp[step - 1].wait_recv()
            YP[rd] = (YP[rd].astype(F32) + RR[step - 2].astype(F32)).astype(BF)
            lcp[step - 1].wait_recv()
            YP[ld] = (YP[ld].astype(F32) + RL[step - 2].astype(F32)).astype(BF)
        if step == 1:
            rs, rt = YP.at[rd, :, 0:1024], RR.at[0, :, 0:1024]
            ls, lt = YP.at[ld, :, 1024:2048], RL.at[0, :, 1024:2048]
        else:
            rs, rt = YP.at[rd], RR.at[step - 1]
            ls, lt = YP.at[ld], RL.at[step - 1]
        rcp[step] = cop.send(rs, rt, y_s.at[0, step - 1], y_r.at[0, step - 1], ydev(1))
        lcp[step] = cop.send(ls, lt, y_s.at[1, step - 1], y_r.at[1, step - 1], ydev(-1))
    rcp[4].wait_recv()
    lcp[4].wait_recv()
    EO[z] = (YP[y].astype(F32) + RR[3].astype(F32) + RL[3].astype(F32)).astype(BF)

    ering = Ring(
        cop, lambda slot, k: EO.at[slot, :, k * 512:(k + 1) * 512], z, zdev(1), zdev(-1), e_s, e_r, 4
    )
    for step in (1, 2, 3, 4):
        ering.forward(step)
    ering.finish()
    for n in range(4):
        cols = slice(n * 512, (n + 1) * 512)
        e = EO[:, :, cols].reshape(NZ * FCAP, 512)
        out[:, cols] = (RES[:, cols] + nn(FG[0], e) + nn(FG[1], e)).astype(BF)

    cop.drain()
    for d in range(1, NX):

        @pl.when(x >= d)
        def _():
            pltpu.make_async_remote_copy(
                src_ref=q, dst_ref=QB.at[d], send_sem=q_s.at[d], recv_sem=q_r.at[d],
                device_id=xdev(-d), device_id_type=MESH,
            ).wait_send()

        @pl.when(x + d < NX)
        def _():
            for src, dst, i in ((OS, OB, 0), (SS, SB, 1)):
                pltpu.make_async_remote_copy(
                    src_ref=src.at[d], dst_ref=dst.at[d], send_sem=o_s.at[d, i], recv_sem=o_r.at[d, i],
                    device_id=xdev(d), device_id_type=MESH,
                ).wait_send()


def shards(
    residual, queries, keys, values, attn_routes, attn_gates, out_weight, norm_gain,
    ffn_routes, ffn_gates, w_gate, w_up, w_down,
):
    q = jnp.transpose(queries[0], (1, 0, 2)).reshape(2 * TOK, HEAD)
    kv = jnp.stack([keys[0], values[0]])
    meta = jnp.concatenate(
        [attn_routes[0].astype(F32), attn_gates[0], ffn_routes[0].astype(F32), ffn_gates[0]], axis=1
    ).T
    w = out_weight[0]
    wo = jnp.concatenate([w[:512], w[512:]], axis=1)
    zero = jnp.zeros((D, 16), BF)
    gate, up = w_gate[0], w_up[0]
    gu = jnp.concatenate([gate[:, :128], gate[:, 128:], zero, up[:, 128:], zero, up[:, :128]], axis=1)
    vm = pl.BlockSpec(memory_space=pltpu.VMEM)
    hbm = pl.BlockSpec(memory_space=pl.ANY)
    dma = lambda *s: pltpu.SemaphoreType.DMA(s)
    vb = lambda *s: pltpu.VMEM(s, BF)
    vf = lambda *s: pltpu.VMEM(s, F32)
    out = pl.pallas_call(
        layer_kernel,
        name="layer",
        out_shape=jax.ShapeDtypeStruct((TOK, D), BF),
        in_specs=[vm, vm, vm, vm, vm, hbm, hbm, hbm],
        out_specs=vm,
        scratch_shapes=[
            vb(NY, 2, TOK, HEAD),
            vb(NX, 2 * TOK, HEAD),
            vb(NX, HEAD, 2 * TOK),
            vf(NX, 8, 2 * TOK),
            vb(NX, HEAD, 2 * TOK),
            vf(NX, 8, 2 * TOK),
            vb(NX, NY, 512, HEAD),
            vb(NX, D, 384),
            vb(NX, 176, D),
            vb(NZ, ACAP, HEAD),
            vb(NZ, ACAP, HEAD),
            vb(NZ, ACAP, D),
            vb(2, TOK, NZ * ACAP),
            vb(2, TOK, NZ * FCAP),
            vb(NY, FCAP, D),
            vb(NY, FCAP, D),
            vb(4, FCAP, D),
            vb(4, FCAP, D),
            vb(NZ, FCAP, D),
            vf(TOK, D),
            dma(3),
            dma(2, 4, 2), dma(2, 4, 2),
            dma(NX), dma(NX),
            dma(NX, 2), dma(NX, 2),
            dma(3), dma(3),
            dma(2, 4, 2), dma(2, 4, 2),
            dma(8), dma(8),
            dma(2, 4), dma(2, 4),
            dma(3, 2), dma(3, 2),
            dma(8), dma(8),
            dma(2, 4, 4), dma(2, 4, 4),
            dma(2, 4, 4), dma(2, 4, 4),
            dma(2, 4), dma(2, 4),
            dma(2, 4, 4), dma(2, 4, 4),
        ],
        compiler_params=pltpu.CompilerParams(
            collective_id=0, has_side_effects=True, vmem_limit_bytes=56 * 1024 * 1024
        ),
    )(meta, residual[0], q, kv, norm_gain.reshape(1, D), wo, gu, w_down[0])
    return out[None]


def solution(mesh):
    in_specs = (
        P("dp", "ctx", None),
        P("dp", "ctx", None, "exp"),
        P("dp", "ctx", "exp"),
        P("dp", "ctx", "exp"),
        P("dp", "ctx", None),
        P("dp", "ctx", None),
        P("exp", None, "ctx"),
        P(),
        P("dp", "ctx", None),
        P("dp", "ctx", None),
        P("exp", None, "ctx"),
        P("exp", None, "ctx"),
        P("exp", "ctx", None),
    )
    out_specs = P("dp", "ctx", None)
    return jax.shard_map(shards, mesh=mesh, in_specs=in_specs, out_specs=out_specs, check_vma=False)
```

time: 778 us -> 147 us (0.19)
  waiting for transfers between devices: 700 us -> 0 us
  Pallas kernels: 0 us -> 135 us
  matrix products: 20.8 us -> 0 us
  other arithmetic: 21.9 us -> 1.99 us
  between operations: 13.7 us -> 0.16 us
  starting transfers between devices: 7.8 us -> 0 us
    all_gather x4 -> x0, waiting for transfers between devices: 309 us -> none  [the longest x1 82.9 us: shards(): shard_rows = lax.all_gather(ffn_in, 'ctx', axis=0, tiled=True)]
    reduce_scatter x1 -> x0, waiting for transfers between devices: 224 us -> none  [shards(): lax.psum_scatter(partial_sums.astype(jnp.bfloat16), 'ctx', scatter_dimens...]
    psum x2 -> x0, waiting for transfers between devices: 157 us -> none  [the longest x1 79.5 us: shards(): lax.psum(ffn_part.astype(jnp.bfloat16), 'exp').astype(jnp.float32)]
    pallas_call x0 -> x1, Pallas kernels: none -> 135 us  [shards(): pl.pallas_call(layer_kernel, name='layer', out_shape=jax.ShapeDtypeStruct...]
    dot_general x5 -> x0, matrix products: 20.8 us -> none  [the longest x1 6.86 us: shards(): jnp.dot(hidden, w_down[0], preferred_element_type=jnp.float32)]
    reduce_sum x6 -> x0, other arithmetic: 13.9 us -> none  [the longest x1 6.38 us: shards(): jnp.sum((ffn_picked * ffn_weight[:, None]).reshape(tok_dev, 2, width), ax...]
    all_to_all x1 -> x0, waiting for transfers between devices: 7.86 us -> none  [shards(): lax.all_to_all(packed, 'exp', split_axis=0, concat_axis=2, tiled=True)[0]]
  transfers between devices with their start and end apart: 8 -> 0, of which waited for: 8 -> 0; matrix products, arithmetic and copies ran while one was open for 2% -> 0% of each run, Pallas kernels for 0% -> 0%
where the time goes in v1:
time: 147 us
  Pallas kernels  135 us (92%)
  local copies, waits for them, and re-layouts  9.09 us (6%)
  other arithmetic  1.99 us (1%)
    pallas_call x1, Pallas kernels, shards(): pl.pallas_call(layer_kernel, name='layer', out_shape=jax.ShapeDtypeStruct...  135 us
    unnamed x23, local copies, waits for them, and re-layouts  4.17 us
    concatenate x1, local copies, waits for them, and re-layouts, shards(): jnp.concatenate([gate[:, :128], gate[:, 128:], zero, up[:, 128:], zero, u...  4.12 us

profile of v1, /device:TPU:6, one launch (start us, length us, event | category | flops | bytes accessed | tf_op | source)
XLA Modules:
  0.0 146.6 jit_solution(2425450394331237255)
XLA Ops:
  0.0 1.5 %copy.18 = bf16[1,2048,176]{2,1,0:T(8,128)(2,1)S(1)} copy(bf16[1,2048,176]{1,2,0:T(8,128)(2,1)} %param.24) | data formatting | bytes 1441792 | tf_op args[11]
  1.6 0.0 copy-done
  1.6 0.5 copy.17
  2.1 0.1 broadcast_in_dim.6
  2.2 0.0 copy-start.1
  2.2 0.0 copy-start.5
  2.2 0.0 copy-start.6
  2.2 0.0 copy-start.7
  2.2 0.0 copy-start.8
  2.2 0.0 copy-start.2
  2.3 0.0 copy-start.3
  2.3 0.0 copy-start.4
  2.3 4.1 %concatenate.11.gu = bf16[2048,384]{1,0:T(8,128)(2,1)} concatenate(bf16[2048,176]{1,0:T(8,128)(2,1)S(1)} %bitcast.22, bf16[2048,16]{1,0:T(8,128)(2,1)S(1)} %broadcast_in_dim.6, bf16[2048,48]{1,0:T(8,128)(2,1)S(1)} %slice.27, bf16[2048,16]{1,0:T(8,128)(2,1)S(1)} %broadcast_in_dim.6, bf16[2048,128]{1,0:T(8,128)(2,1)S(1)} %slice.28), dimensions={1} | concatenate | bytes 3145728 | tf_op jit(solution)/shard_map/concatenate | solution.py:490
  6.4 0.0 copy-done.1
  6.4 0.1 copy.19
  6.5 0.1 copy.20
  6.7 0.8 pad_maximum_fusion.wo
  7.5 0.0 copy-done.5
  7.5 0.6 maximum_bitcast_fusion.meta
  8.1 0.6 copy.14
  8.7 0.0 copy-done.3
  8.7 0.6 pad_maximum_fusion.1.kv
  9.4 135.3 %layer.1 = bf16[128,2048]{1,0:T(8,128)(2,1)} custom-call(f32[8,128]{1,0:T(8,128)} %maximum_bitcast_fusion.meta, bf16[128,2048]{1,0:T(8,128)(2,1)} %bitcast.27, bf16[256,128]{1,0:T(8,128)(2,1)} %bitcast.28, bf16[2,128,128]{2,1,0:T(8,128)(2,1)} %pad_maximum_fusion.1.kv, f32[1,2048]{1,0:T(1,128)} %bitcast.30, bf16[512,128]{1,0:T(8,128)(2,1)} %pad_maximum_fusion.wo, ...), custom_call_target="tpu_custom_call" | custom-call | tf_op jit(solution)/shard_map/layer/pallas_call | solution.py:496
  144.7 1.9 %copy.22 = bf16[1,128,2048]{2,1,0:T(8,128)(2,1)} copy(bf16[1,128,2048]{2,1,0:T(8,128)(2,1)} %bitcast.23) | data formatting | bytes 1048576
  (10 shorter events, 0.1 us)
Async XLA Ops:
  0.0 1.6 %copy-start = (bf16[1,2048,176]{1,2,0:T(8,128)(2,1)S(1)}, bf16[1,2048,176]{1,2,0:T(8,128)(2,1)}, u32[]{:S(2)}) copy-start(bf16[1,2048,176]{1,2,0:T(8,128)(2,1)} %param.23) | copy-start | bytes 2162692
  2.2 4.2 %copy-start.1 = (bf16[1,1024,64]{1,2,0:T(8,128)(2,1)S(1)}, bf16[1,1024,64]{1,2,0:T(8,128)(2,1)}, u32[]{:S(2)}) copy-start(bf16[1,1024,64]{1,2,0:T(8,128)(2,1)} %param.19) | copy-start | bytes 393220
  2.2 5.3 %copy-start.5 = (s32[1,128,2]{1,2,0:T(2,128)S(1)}, s32[1,128,2]{1,2,0:T(2,128)}, u32[]{:S(2)}) copy-start(s32[1,128,2]{1,2,0:T(2,128)} %param.21) | copy-start | bytes 3076
  2.2 5.2 %copy-start.6 = (s32[1,128,2]{1,2,0:T(2,128)S(1)}, s32[1,128,2]{1,2,0:T(2,128)}, u32[]{:S(2)}) copy-start(s32[1,128,2]{1,2,0:T(2,128)} %param.17) | copy-start | bytes 3076
  2.2 5.2 %copy-start.7 = (f32[1,128,2]{1,2,0:T(2,128)S(1)}, f32[1,128,2]{1,2,0:T(2,128)}, u32[]{:S(2)}) copy-start(f32[1,128,2]{1,2,0:T(2,128)} %param.22) | copy-start | bytes 3076
  2.2 5.2 %copy-start.8 = (f32[1,128,2]{1,2,0:T(2,128)S(1)}, f32[1,128,2]{1,2,0:T(2,128)}, u32[]{:S(2)}) copy-start(f32[1,128,2]{1,2,0:T(2,128)} %param.18) | copy-start | bytes 3076
  2.2 5.8 %copy-start.2 = (bf16[1,128,2,128]{3,2,1,0:T(2,128)(2,1)S(1)}, bf16[1,128,2,128]{3,2,1,0:T(2,128)(2,1)}, u32[]{:S(2)}) copy-start(bf16[1,128,2,128]{3,2,1,0:T(2,128)(2,1)} %param.14) | copy-start | bytes 196612
  2.3 6.5 %copy-start.3 = (bf16[1,128,128]{2,1,0:T(8,128)(2,1)S(1)}, bf16[1,128,128]{2,1,0:T(8,128)(2,1)}, u32[]{:S(2)}) copy-start(bf16[1,128,128]{2,1,0:T(8,128)(2,1)} %param.16) | copy-start | bytes 98308
  2.3 6.4 %copy-start.4 = (bf16[1,128,128]{2,1,0:T(8,128)(2,1)S(1)}, bf16[1,128,128]{2,1,0:T(8,128)(2,1)}, u32[]{:S(2)}) copy-start(bf16[1,128,128]{2,1,0:T(8,128)(2,1)} %param.15) | copy-start | bytes 98308

commit v2 on v0

v2 whole, which is shorter than its diff:
```python
import functools
import math

import jax
import jax.numpy as jnp
from jax import lax
from jax.experimental import pallas as pl
from jax.experimental.pallas import tpu as pltpu
from jax.sharding import PartitionSpec as P

MESH = pl.DeviceIdType.MESH
BF = jnp.bfloat16
F32 = jnp.float32
NX, NY, NZ = 4, 8, 8
TOK = 128
D = 2048
HEAD = 128
ACAP = 48
FCAP = 32
NEG = -1e30


def nt(a, b):
    return lax.dot_general(a, b, (((1,), (1,)), ((), ())), preferred_element_type=F32)


def tn(a, b):
    return lax.dot_general(a, b, (((0,), (0,)), ((), ())), preferred_element_type=F32)


def nn(a, b):
    return jnp.dot(a, b, preferred_element_type=F32)


def wrap(v, n):
    return lax.rem(v + 2 * n, n)


class Copy:
    def __init__(self, src, dst, ssem, rsem, dev, sends=None, gets=None):
        self.cp = pltpu.make_async_remote_copy(
            src_ref=src, dst_ref=dst, send_sem=ssem, recv_sem=rsem, device_id=dev, device_id_type=MESH
        )
        self.sends, self.gets = sends, gets
        self.done = False

    def _when(self, cond, act):
        if cond is None:
            act()
        else:
            pl.when(cond)(act)

    def start(self):
        self._when(self.sends, self.cp.start)

    def wait_recv(self):
        self.done = True
        self._when(self.gets, self.cp.wait_recv)

    def wait_send(self):
        self._when(self.sends, self.cp.wait_send)


class Copies:
    def __init__(self):
        self.sent = []

    def send(self, src, dst, ssem, rsem, dev, sends=None, gets=None):
        cp = Copy(src, dst, ssem, rsem, dev, sends, gets)
        cp.start()
        self.sent.append(cp)
        return cp

    def drain(self):
        for cp in self.sent:
            if not cp.done:
                cp.wait_recv()
        for cp in self.sent:
            cp.wait_send()


class Ring:
    def __init__(self, copies, at, pos, right, left, ssem, rsem, chunks):
        self.copies, self.at, self.pos = copies, at, pos
        self.devs = (right, left)
        self.ssem, self.rsem, self.chunks = ssem, rsem, chunks
        self.cps = {}

    def carries(self, way, step, j):
        return step < 4 or (j < self.chunks // 2) == (way == 0)

    def slot(self, way, step):
        return wrap(self.pos - step if way == 0 else self.pos + step, 8)

    def start(self, step, j):
        for way in (0, 1):
            if self.carries(way, step, j):
                slot = self.slot(way, step - 1)
                src = self.at(slot, j)
                self.cps[way, step, j] = self.copies.send(
                    src, self.at(slot, j), self.ssem.at[way, step - 1, j], self.rsem.at[way, step - 1, j], self.devs[way]
                )

    def wait(self, step, j):
        for way in (0, 1):
            if self.carries(way, step, j):
                self.cps[way, step, j].wait_recv()

    def forward(self, step, js=None):
        for j in range(self.chunks) if js is None else js:
            if step > 1:
                self.wait(step - 1, j)
            self.start(step, j)

    def finish(self):
        for j in range(self.chunks):
            self.wait(4, j)


class Two:
    def __init__(self, copies, at, pos, dev, ssem, rsem):
        self.copies, self.at, self.pos, self.dev = copies, at, pos, dev
        self.ssem, self.rsem = ssem, rsem
        self.cps = {}

    def _send(self, way, n, ref, k):
        sign = 1 if way == 0 else -1
        self.cps[way, n] = self.copies.send(
            ref, ref, self.ssem.at[way, n - 1], self.rsem.at[way, n - 1], self.dev(sign * k)
        )

    def start(self):
        for k in (2, 1):
            for way in (0, 1):
                self._send(way, k, self.at(self.pos, None), k)

    def forward(self):
        for way in (0, 1):
            self.cps[way, 2].wait_recv()
        for way in (0, 1):
            slot = wrap(self.pos - 2 if way == 0 else self.pos + 2, 8)
            self._send(way, 4, self.at(slot, way), 2)
            self._send(way, 3, self.at(slot, None), 1)

    def wait(self, *ns):
        for n in ns:
            for way in (0, 1):
                self.cps[way, n].wait_recv()


class Rounds:
    def __init__(self, copies, at, pos, dev, ssem, rsem, chunks):
        self.copies, self.at, self.pos, self.dev = copies, at, pos, dev
        self.ssem, self.rsem, self.chunks = ssem, rsem, chunks
        self.cps = {}

    def _send(self, way, n, j, slot, k):
        ref = self.at(slot, j)
        self.cps[way, n, j] = self.copies.send(
            ref, ref, self.ssem.at[way, n - 1, j], self.rsem.at[way, n - 1, j],
            self.dev(k if way == 0 else -k),
        )

    def start(self, *js):
        for j in js:
            for k in (2, 1):
                for way in (0, 1):
                    self._send(way, k, j, self.pos, k)

    def forward(self, *js):
        for j in js:
            for way in (0, 1):
                self.cps[way, 2, j].wait_recv()
                slot = wrap(self.pos - 2 if way == 0 else self.pos + 2, 8)
                if (j < self.chunks // 2) == (way == 0):
                    self._send(way, 4, j, slot, 2)
                self._send(way, 3, j, slot, 1)

    def wait(self, *js):
        for j in js:
            for n in (1, 3, 4):
                for way in (0, 1):
                    if (way, n, j) in self.cps:
                        self.cps[way, n, j].wait_recv()


def layer_kernel(
    res, q, kk, vv, ar, ag, fr, fg, gain, wo, wg, wu, wd, out,
    RB, QV, AR, AG, FR, FGT, GN, KV, QB, OA, ML, OB, SB, OS, SS, WO, W, PK, ER, PR, PT, MG, FG, XN, XR, YP, RR, RL,
    EO, RES,
    l_s, kv_s, kv_r, q_s, q_r, o_s, o_r, wb_s, wb_r, wz_s, wz_r, wc_s, wc_r,
    fx_s, fx_r, fa_s, fa_r, fc_s, fc_r, a_s, a_r, p_s, p_r, x_s, x_r, y_s, y_r, e_s, e_r,
):
    j = lax.axis_index("dp")
    c = lax.axis_index("ctx")
    z = lax.axis_index("exp")
    x = c // NY
    y = c % NY
    cop = Copies()

    def xdev(k):
        return (j, wrap(x + k, NX) * NY + y, z)

    def ydev(k):
        return (j, x * NY + wrap(y + k, NY), z)

    def zdev(k):
        return (j, c, wrap(z + k, NZ))

    sib = (1 - j, c, z)

    def part(n, i):
        return pl.ds(pl.multiple_of(i * n, n), n)

    barrier = pltpu.get_barrier_semaphore()
    partners = [xdev(k) for k in (1, 2, 3)] + [ydev(k) for k in (1, 2, -2, -1)] + [zdev(k) for k in range(1, 8)] + [sib]
    for dev in partners:
        pl.semaphore_signal(barrier, inc=1, device_id=dev, device_id_type=MESH)

    local = [
        (kk, KV.at[y, 0]), (vv, KV.at[y, 1]), (q, QV),
        (ar, AR), (ag, AG), (fr, FR), (fg, FGT),
        (res, RB), (gain, GN),
        (wo.at[:, part(512, j)], WO.at[x, y, :, part(512, j)]),
        (wg, W.at[0, x]), (wu, W.at[1, x]), (wd, W.at[2, x]),
    ]
    own_w = [pltpu.make_async_copy(src, dst, l_s.at[i]) for i, (src, dst) in enumerate(local)]

    def wait_local(*ids):
        for i in ids:
            own_w[i].wait()

    for cp in own_w:
        cp.start()
    pl.semaphore_wait(barrier, len(partners))

    lanes = part(512, j)
    wait_local(0, 1)
    kvring = Two(
        cop, lambda slot, h: KV.at[slot] if h is None else KV.at[slot, h], y, ydev, kv_s, kv_r
    )
    kvring.start()
    qcp = {
        d: cop.send(q, QB.at[d], q_s.at[d], q_r.at[d], xdev(-d), sends=x >= d, gets=x + d < NX)
        for d in (3, 2, 1)
    }

    def block(slot, h):
        if h is None:
            return WO.at[x, slot, :, lanes]
        return WO.at[x, slot, 32 * h:32 * h + 32, lanes]

    wb = Two(cop, block, y, ydev, wb_s, wb_r)
    wz = {}
    wcs = []

    def to_sibling(*slots):
        for slot in slots:
            n = len(wcs)
            ref = WO.at[slot, :, :, lanes]
            wcs.append(cop.send(ref, ref, wc_s.at[n], wc_r.at[n], sib))

    def along_x(*ns):
        for n in ns:
            slot = wrap(y + n, NY)
            for way, step in ((0, 1), (1, -1)):
                wz[way, 0, n] = cop.send(
                    wo.at[:, lanes] if n == 0 else WO.at[x, slot, :, lanes], WO.at[x, slot, :, lanes],
                    wz_s.at[way, 0, n], wz_r.at[way, 0, n], xdev(step),
                )

    def along_x_again(*ns):
        for n in ns:
            slot = wrap(y + n, NY)
            for way, step in ((0, 1), (1, -1)):
                wz[way, 0, n].wait_recv()
                ref = WO.at[wrap(x - step, NX), slot, 32 * way:32 * way + 32, lanes]
                wz[way, 1, n] = cop.send(ref, ref, wz_s.at[way, 1, n], wz_r.at[way, 1, n], xdev(step))

    along_x(0)

    quarter = [pl.ds(pl.multiple_of(j * 1024 + h * 512, 512), 512) for h in (0, 1)]
    fx = {}

    def send_weights(which):
        for turn in (0, 1):
            for way, step in ((0, 1), (1, -1)):
                h = turn if way == 0 else 1 - turn
                for i in which:
                    fx[way, i, h] = cop.send(
                        (wg, wu, wd)[i].at[:, quarter[h]], W.at[i, x, :, quarter[h]],
                        fx_s.at[way, i, h], fx_r.at[way, i, h], xdev(step),
                    )

    fa = {}

    def forward_weights(which):
        for way, step in ((0, 1), (1, -1)):
            slot = wrap(x - step, NX)
            for i in which:
                fx[way, i, way].wait_recv()
                ref = W.at[i, slot, :, quarter[way]]
                fa[way, i] = cop.send(ref, ref, fa_s.at[way, i], fa_r.at[way, i], xdev(step))

    fcs = []

    def weights_to_sibling(n, which, slot):
        for i in which:
            ref = W.at[i, slot, :, part(1024, j)]
            fcs.append(cop.send(ref, ref, fc_s.at[n, i], fc_r.at[n, i], sib))

    def near_to_sibling(which):
        for way, step in ((0, 1), (1, -1)):
            for i in which:
                fx[way, i, 1 - way].wait_recv()
            weights_to_sibling(way, which, wrap(x - step, NX))

    def far_to_sibling(which):
        for i in which:
            for way in (0, 1):
                fa[way, i].wait_recv()
        weights_to_sibling(2, which, wrap(x + 2, NX))

    send_weights((0,))

    factor = math.log2(math.e) / math.sqrt(HEAD)

    def absorb(d, blocks, first=False, last=False):
        queries = QV[...] if d == 0 else QB[d]
        ks = jnp.concatenate([KV[b, 0] for b in blocks], axis=0)
        vs = jnp.concatenate([KV[b, 1] for b in blocks], axis=0)
        s = nt(ks, queries) * factor
        if d == 0:
            row = lax.broadcasted_iota(jnp.int32, (TOK, 2 * TOK), 0)
            qpos = y * TOK + lax.shift_right_logical(
                lax.broadcasted_iota(jnp.int32, (TOK, 2 * TOK), 1), 1
            )
            allowed = jnp.concatenate([row + b * TOK - qpos for b in blocks], axis=0) <= 0
            s = jnp.where(allowed, s, NEG)
        m = jnp.max(s, axis=0, keepdims=True)
        if not first:
            old = ML[d, 0:1, :]
            m = jnp.maximum(m, old)
        p = jnp.exp2(s - m)
        l = jnp.sum(p, axis=0, keepdims=True)
        o = tn(vs, p.astype(BF))
        if not first:
            shrink = jnp.exp2(old - m)
            l = l + ML[d, 1:2, :] * shrink
            o = o + OA[d] * shrink
        if last:
            return o, m, l
        ML[d, 0:1, :] = m
        ML[d, 1:2, :] = l
        OA[d] = o

    def absorb_later(blocks, first=False):
        for d in range(1, NX):

            @pl.when(x + d < NX)
            def _():
                absorb(d, blocks, first)

    def pair(step):
        return [wrap(y - step, NY), wrap(y + step, NY)]

    wait_local(2, 9)
    absorb(0, [y], first=True)
    wb.start()

    wait_local(3, 4, 5, 6)
    upper = (
        lax.broadcasted_iota(jnp.int32, (256, 256), 0) < lax.broadcasted_iota(jnp.int32, (256, 256), 1)
    ).astype(F32).astype(BF)

    def ranks(route):
        eid = lax.broadcasted_iota(jnp.int32, (8, 256), 0).astype(F32)
        onehot = (eid == route).astype(F32)
        before = nn(onehot.astype(BF), upper)
        return jnp.sum(before * onehot, axis=0, keepdims=True)

    def iota0(rows, cols):
        return lax.broadcasted_iota(jnp.int32, (rows, cols), 0).astype(F32)

    def gate_table(slot, gates, rows):
        rid = iota0(rows, TOK)
        t = jnp.where(rid == slot[:, :TOK], gates[0:1, :], 0.0) + jnp.where(
            rid == slot[:, TOK:], gates[1:2, :], 0.0
        )
        t = t.T
        hi = t.astype(BF)
        return hi, (t - hi.astype(F32)).astype(BF)

    aroute = AR[...].astype(F32)
    aroute = jnp.concatenate([aroute[0:1, :], aroute[1:2, :]], axis=1)
    arank = ranks(aroute)
    by_slot = (iota0(8 * ACAP, 256) == aroute * ACAP + arank).astype(F32).astype(BF)
    src = lax.broadcasted_iota(jnp.int32, (256, 256), 0)
    dst = 2 * jnp.bitwise_and(src, TOK - 1) + lax.shift_right_logical(src, 7)
    swap = (lax.broadcasted_iota(jnp.int32, (256, 256), 1) == dst).astype(F32).astype(BF)
    disp = nn(by_slot, swap).astype(BF)
    main = aroute * 32 + arank
    extra = 256 + aroute * 16 + (arank - 32)
    agates = AG[...]
    for i in range(2):
        MG[2 * i], MG[2 * i + 1] = gate_table(jnp.where(arank < 32, main, extra + 8 * i), agates, 384)

    froute = FR[...].astype(F32)
    froute = jnp.concatenate([froute[0:1, :], froute[1:2, :]], axis=1)
    fslot = froute * FCAP + ranks(froute)
    FG[0], FG[1] = gate_table(fslot, FGT[...], 8 * FCAP)
    mine = iota0(FCAP, TOK) + (z * FCAP).astype(F32)
    sel = ((mine == fslot[:, :TOK]).astype(F32) + (mine == fslot[:, TOK:]).astype(F32)).astype(BF)

    kvring.forward()
    kvring.wait(1)
    near = pair(1) + pair(2)
    absorb(0, near)
    for d in range(1, NX):
        qcp[d].wait_recv()
    absorb_later([y] + near, first=True)
    wb.forward()
    wb.wait(1)
    along_x(1, 7, 2, 6)
    kvring.wait(3, 4)
    ocp = []
    final = pair(3) + [wrap(y + 4, NY)]
    for d in (3, 2, 1):

        @pl.when(x + d < NX)
        def _():
            o, m, l = absorb(d, final, last=True)
            OS[d] = o.astype(BF)
            SS[d] = jnp.concatenate([m, l, jnp.zeros((6, 2 * TOK), F32)], axis=0)

        for src, dst, i in ((OS, OB, 0), (SS, SB, 1)):
            ocp.append(
                cop.send(
                    src.at[d], dst.at[d], o_s.at[d, i], o_r.at[d, i], xdev(d),
                    sends=x + d < NX, gets=x >= d,
                )
            )
    o, m, l = absorb(0, final, last=True)
    wb.wait(3, 4)
    along_x(3, 5, 4)
    to_sibling(x)
    along_x_again(0, 1, 7, 2, 6)
    for cp in ocp:
        cp.wait_recv()
    tops = [jnp.where(x >= d, SB[d, 0:1, :], NEG) for d in range(1, NX)]
    top = m
    for t in tops:
        top = jnp.maximum(top, t)
    f = jnp.exp2(m - top)
    o = o * f
    l = l * f
    for d in range(1, NX):
        f = jnp.exp2(tops[d - 1] - top)
        o = o + jnp.where(x >= d, OB[d].astype(F32), 0.0) * f
        l = l + jnp.where(x >= d, SB[d, 1:2, :], 0.0) * f
    attended = (o / l).astype(BF)

    PK[...] = nt(disp, attended).astype(BF).reshape(NZ, ACAP, HEAD)
    acps = [cop.send(PK.at[wrap(z + k, NZ)], ER.at[z], a_s.at[k], a_r.at[k], zdev(k)) for k in range(1, NZ)]
    ER[z] = PK[z]
    along_x_again(3, 5, 4)
    to_sibling(wrap(x - 1, NX), wrap(x + 1, NX))
    forward_weights((0,))
    send_weights((1, 2))
    for cp in acps:
        cp.wait_recv()
    lhs = jnp.concatenate([ER[h] for h in range(NZ)], axis=1)
    order = [x, wrap(x - 1, NX), wrap(x + 1, NX), wrap(x + 2, NX)]
    real = [part(512, b) for b in order]
    ends = {}

    def project(n):
        wcs[n].wait_recv()
        r = nt(lhs, WO[order[n]].reshape(512, 1024))
        PR[z, :, n * 512:(n + 1) * 512] = r[0:32].astype(BF)
        ends[n] = r[32:40]
        if n % 2 == 1:
            k = n // 2
            PT[z, :, k * 512:(k + 1) * 512] = jnp.concatenate([ends[n - 1], ends[n]], axis=0).astype(BF)
            pring.start(2 * k, 2 * k + 1)

    def wide(slot, k):
        h = (k // 2) * 1024
        return PR.at[slot, :, h:h + 1024] if k % 2 == 0 else PT.at[slot, :, h // 2:h // 2 + 512]

    pring = Rounds(cop, wide, z, zdev, p_s, p_r, 4)
    A, B = (0, 1), (2, 3)
    project(0)
    project(1)
    project(2)
    wait_local(7, 8)
    tables = [nn(sel, MG[i]).astype(BF) for i in range(4)]
    picked = [nn(sel, RB[:, real[n]]) for n in range(4)]
    pring.forward(*A)
    for way in (0, 1):
        for n in range(NY):
            wz[way, 1, n].wait_recv()
    to_sibling(wrap(x + 2, NX))
    project(3)
    pring.forward(*B)

    def projected(n):
        t = (n // 2) * 512
        return jnp.concatenate(
            [
                PR[:, :, n * 512:(n + 1) * 512].reshape(256, 512),
                PT[:, :, t:t + 512].reshape(128, 512),
            ],
            axis=0,
        )

    xring = Rounds(
        cop, lambda slot, k: XN.at[slot, :, k * 512:(k + 1) * 512], y, ydev, x_s, x_r, 4
    )

    def pick(group):
        pring.wait(*group)
        for n in group:
            rows = projected(n)
            h = 2 * (n % 2)
            XN[y, :, n * 512:(n + 1) * 512] = (
                picked[n] + nn(tables[h], rows) + nn(tables[h + 1], rows)
            ).astype(BF)
            xring.start(n)

    pick(A)
    pick(B)
    xring.forward(*A)

    def normalise(slot):
        v = XN[slot].astype(F32)
        scale = lax.rsqrt(jnp.mean(v * v, axis=1, keepdims=True) + 1e-6)
        for n in range(4):
            XR[slot, :, real[n]] = (v[:, n * 512:(n + 1) * 512] * scale * GN[:, real[n]]).astype(BF)

    near_to_sibling((0,))
    forward_weights((1, 2))
    near_to_sibling((1, 2))
    normalise(y)
    xring.forward(*B)
    for n in range(4):
        rows = projected(n)
        h = 2 * (n % 2)
        RES[:, real[n]] = RB[:, real[n]].astype(F32) + nn(MG[h], rows) + nn(MG[h + 1], rows)
    far_to_sibling((0,))
    xring.wait(*A, *B)
    for slot in pair(1) + pair(2) + pair(3) + [wrap(y + 4, NY)]:
        normalise(slot)
    wait_local(10, 11, 12)
    for cp in fcs:
        cp.wait_recv()
    fcs.clear()
    far_to_sibling((1, 2))
    for cp in fcs:
        cp.wait_recv()
    fcs.clear()
    rows = XR[...].reshape(NY * FCAP, D)
    hidden = []
    for n in (0, 256, 512):
        size = min(256, 704 - n)
        g = nt(rows, W[0].reshape(704, D)[n:n + size])
        u = nt(rows, W[1].reshape(704, D)[n:n + size])
        hidden.append((g / (1.0 + jnp.exp(-g)) * u).astype(BF))
    hidden = jnp.concatenate(hidden, axis=1)

    def cut(ref, k, n):
        return ref.at[k, :, n * 512:(n + 1) * 512]

    hop = {}

    def pass_on(way, near, n, dest, k):
        sign = 1 if way == 0 else -1
        hop[way, near, n] = cop.send(
            cut(YP, wrap(y + sign * dest, NY), n), cut((RR, RL)[way], near, n),
            y_s.at[way, near, n], y_r.at[way, near, n], ydev(sign * k),
        )

    for n in range(4):
        cols = slice(n * 512, (n + 1) * 512)
        YP[:, :, cols] = nn(hidden, W[2, :, :, cols].reshape(704, 512)).astype(BF).reshape(NY, FCAP, 512)
        pass_on(n // 2, 3, n, 4, 2)
        for way in (0, 1):
            pass_on(way, 2, n, 3, 1)
    for n in range(4):
        cols = slice(n * 512, (n + 1) * 512)
        for way in (0, 1):
            got = (RR, RL)[way]
            dest = wrap(y + 2 if way == 0 else y - 2, NY)
            hop[way, 2, n].wait_recv()
            share = YP[dest, :, cols].astype(F32) + got[2, :, cols].astype(F32)
            if way == n // 2:
                hop[way, 3, n].wait_recv()
                share = share + got[3, :, cols].astype(F32)
            YP[dest, :, cols] = share.astype(BF)
            pass_on(way, 1, n, 2, 2)
        for way in (0, 1):
            pass_on(way, 0, n, 1, 1)
    ering = Rounds(
        cop, lambda slot, k: EO.at[slot, :, k * 512:(k + 1) * 512], z, zdev, e_s, e_r, 4
    )
    for n in range(4):
        cols = slice(n * 512, (n + 1) * 512)
        total = YP[y, :, cols].astype(F32)
        for way in (0, 1):
            for near in (0, 1):
                hop[way, near, n].wait_recv()
                total = total + (RR, RL)[way][near, :, cols].astype(F32)
        EO[z, :, cols] = total.astype(BF)
        ering.start(n)
    ering.forward(*A, *B)
    for n in range(4):
        cols = slice(n * 512, (n + 1) * 512)
        ering.wait(n)
        e = EO[:, :, cols].reshape(NZ * FCAP, 512)
        out[:, cols] = (RES[:, cols] + nn(FG[0], e) + nn(FG[1], e)).astype(BF)

    cop.drain()


def shards(
    residual, queries, keys, values, attn_routes, attn_gates, out_weight, norm_gain,
    ffn_routes, ffn_gates, w_gate, w_up, w_down,
):
    hbm = pl.BlockSpec(memory_space=pl.ANY)
    dma = lambda *s: pltpu.SemaphoreType.DMA(s)
    vb = lambda *s: pltpu.VMEM(s, BF)
    vf = lambda *s: pltpu.VMEM(s, F32)
    vi = lambda *s: pltpu.VMEM(s, jnp.int32)
    out = pl.pallas_call(
        layer_kernel,
        name="layer",
        out_shape=jax.ShapeDtypeStruct((TOK, D), BF),
        in_specs=[hbm] * 13,
        out_specs=pl.BlockSpec(memory_space=pltpu.VMEM),
        scratch_shapes=[
            vb(TOK, D),
            vb(2 * TOK, HEAD),
            vi(2, TOK), vf(2, TOK), vi(2, TOK), vf(2, TOK),
            vf(1, D),
            vb(NY, 2, TOK, HEAD),
            vb(NX, 2 * TOK, HEAD),
            vf(NX, HEAD, 2 * TOK),
            vf(NX, 8, 2 * TOK),
            vb(NX, HEAD, 2 * TOK),
            vf(NX, 8, 2 * TOK),
            vb(NX, HEAD, 2 * TOK),
            vf(NX, 8, 2 * TOK),
            vb(NX, NY, 64, 1024),
            vb(3, NX, 176, D),
            vb(NZ, ACAP, HEAD),
            vb(NZ, ACAP, HEAD),
            vb(NZ, 32, D),
            vb(NZ, 16, 1024),
            vb(4, TOK, 384),
            vb(2, TOK, NZ * FCAP),
            vb(NY, FCAP, D),
            vb(NY, FCAP, D),
            vb(NY, FCAP, D),
            vb(4, FCAP, D),
            vb(4, FCAP, D),
            vb(NZ, FCAP, D),
            vf(TOK, D),
            dma(13),
            dma(2, 4), dma(2, 4),
            dma(NX), dma(NX),
            dma(NX, 2), dma(NX, 2),
            dma(2, 4), dma(2, 4),
            dma(2, 2, 8), dma(2, 2, 8),
            dma(4), dma(4),
            dma(2, 3, 2), dma(2, 3, 2),
            dma(2, 3), dma(2, 3),
            dma(3, 3), dma(3, 3),
            dma(8), dma(8),
            dma(2, 4, 4), dma(2, 4, 4),
            dma(2, 4, 4), dma(2, 4, 4),
            dma(2, 4, 4), dma(2, 4, 4),
            dma(2, 4, 4), dma(2, 4, 4),
        ],
        compiler_params=pltpu.CompilerParams(
            collective_id=0, has_side_effects=True, vmem_limit_bytes=56 * 1024 * 1024
        ),
    )(
        residual[0], queries[0].reshape(2 * TOK, HEAD), keys[0], values[0],
        attn_routes[0].T, attn_gates[0].T, ffn_routes[0].T, ffn_gates[0].T,
        norm_gain.reshape(1, D), out_weight[0].T, w_gate[0].T, w_up[0].T, w_down[0],
    )
    return out[None]


def solution(mesh):
    in_specs = (
        P("dp", "ctx", None),
        P("dp", "ctx", None, "exp"),
        P("dp", "ctx", "exp"),
        P("dp", "ctx", "exp"),
        P("dp", "ctx", None),
        P("dp", "ctx", None),
        P("exp", None, "ctx"),
        P(),
        P("dp", "ctx", None),
        P("dp", "ctx", None),
        P("exp", None, "ctx"),
        P("exp", None, "ctx"),
        P("exp", "ctx", None),
    )
    out_specs = P("dp", "ctx", None)
    return jax.shard_map(shards, mesh=mesh, in_specs=in_specs, out_specs=out_specs, check_vma=False)
```

time: 778 us -> 116 us (0.15)
  waiting for transfers between devices: 700 us -> 0 us
  Pallas kernels: 0 us -> 114 us
  other arithmetic: 21.9 us -> 0 us
  matrix products: 20.8 us -> 0 us
  between operations: 13.7 us -> 0.01 us
  local copies, waits for them, and re-layouts: 13.7 us -> 1.88 us
  starting transfers between devices: 7.8 us -> 0 us
    all_gather x4 -> x0, waiting for transfers between devices: 309 us -> none  [the longest x1 82.9 us: shards(): shard_rows = lax.all_gather(ffn_in, 'ctx', axis=0, tiled=True)]
    reduce_scatter x1 -> x0, waiting for transfers between devices: 224 us -> none  [shards(): lax.psum_scatter(partial_sums.astype(jnp.bfloat16), 'ctx', scatter_dimens...]
    psum x2 -> x0, waiting for transfers between devices: 157 us -> none  [the longest x1 79.5 us: shards(): lax.psum(ffn_part.astype(jnp.bfloat16), 'exp').astype(jnp.float32)]
    pallas_call x0 -> x1, Pallas kernels: none -> 114 us  [shards(): pl.pallas_call(layer_kernel, name='layer', out_shape=jax.ShapeDtypeStruct...]
    dot_general x5 -> x0, matrix products: 20.8 us -> none  [the longest x1 6.86 us: shards(): jnp.dot(hidden, w_down[0], preferred_element_type=jnp.float32)]
    reduce_sum x6 -> x0, other arithmetic: 13.9 us -> none  [the longest x1 6.38 us: shards(): jnp.sum((ffn_picked * ffn_weight[:, None]).reshape(tok_dev, 2, width), ax...]
    all_to_all x1 -> x0, waiting for transfers between devices: 7.86 us -> none  [shards(): lax.all_to_all(packed, 'exp', split_axis=0, concat_axis=2, tiled=True)[0]]
  transfers between devices with their start and end apart: 8 -> 0, of which waited for: 8 -> 0; matrix products, arithmetic and copies ran while one was open for 2% -> 0% of each run, Pallas kernels for 0% -> 0%
where the time goes in v2:
time: 116 us; the launch traced here: 115 us
  Pallas kernels  114 us (98%)
  local copies, waits for them, and re-layouts  1.88 us (2%)
    pallas_call x1, Pallas kernels, shards(): pl.pallas_call(layer_kernel, name='layer', out_shape=jax.ShapeDtypeStruct...  114 us

profile of v2, /device:TPU:6, one launch (start us, length us, event | category | flops | bytes accessed | tf_op | source)
XLA Modules:
  0.0 115.4 jit_solution(13029304024259368085)
XLA Ops:
  0.0 113.6 %layer.1 = bf16[128,2048]{1,0:T(8,128)(2,1)} custom-call(bf16[128,2048]{1,0:T(8,128)(2,1)} %bitcast.32, bf16[256,128]{1,0:T(8,128)(2,1)} %bitcast.34, bf16[128,128]{1,0:T(8,128)(2,1)} %bitcast.35, bf16[128,128]{1,0:T(8,128)(2,1)} %bitcast.36, s32[2,128]{1,0:T(2,128)} %bitcast.38, f32[2,128]{1,0:T(2,128)} %bitcast.39, s32[2,128]{1,0:T(2,128)} %bitcast.40, ...), custom_call_target="tpu_custom_call" | custom-call | tf_op jit(solution)/shard_map/layer/pallas_call | solution.py:634
  113.6 1.9 %copy.15 = bf16[1,128,2048]{2,1,0:T(8,128)(2,1)} copy(bf16[1,128,2048]{2,1,0:T(8,128)(2,1)} %bitcast.28) | data formatting | bytes 1048576

commit v3 on v2

--- a/solution.py
+++ b/solution.py
@@ -42,7 +42,7 @@
             src_ref=src, dst_ref=dst, send_sem=ssem, recv_sem=rsem, device_id=dev, device_id_type=MESH
         )
         self.sends, self.gets = sends, gets
-        self.done = False
+        self.done = self.left = False
 
     def _when(self, cond, act):
         if cond is None:
@@ -58,7 +58,9 @@
         self._when(self.gets, self.cp.wait_recv)
 
     def wait_send(self):
-        self._when(self.sends, self.cp.wait_send)
+        if not self.left:
+            self.left = True
+            self._when(self.sends, self.cp.wait_send)
 
 
 class Copies:
@@ -75,8 +77,12 @@
         for cp in self.sent:
             if not cp.done:
                 cp.wait_recv()
+        self.flush()
+
+    def flush(self):
         for cp in self.sent:
             cp.wait_send()
+        self.sent = [cp for cp in self.sent if not cp.done]
 
 
 class Ring:
@@ -188,7 +194,7 @@
     res, q, kk, vv, ar, ag, fr, fg, gain, wo, wg, wu, wd, out,
     RB, QV, AR, AG, FR, FGT, GN, KV, QB, OA, ML, OB, SB, OS, SS, WO, W, PK, ER, PR, PT, MG, FG, XN, XR, YP, RR, RL,
     EO, RES,
-    l_s, kv_s, kv_r, q_s, q_r, o_s, o_r, wb_s, wb_r, wz_s, wz_r, wc_s, wc_r,
+    l_s, kv_s, kv_r, q_s, q_r, o_s, o_r, wb_s, wb_r, wy_s, wy_r, wz_s, wz_r, wc_s, wc_r,
     fx_s, fx_r, fa_s, fa_r, fc_s, fc_r, a_s, a_r, p_s, p_r, x_s, x_r, y_s, y_r, e_s, e_r,
 ):
     j = lax.axis_index("dp")
@@ -250,7 +256,15 @@
             return WO.at[x, slot, :, lanes]
         return WO.at[x, slot, 32 * h:32 * h + 32, lanes]
 
+    far = wrap(x + 2, NX)
+
+    def far_block(slot, h):
+        if h is None:
+            return WO.at[far, slot, :, lanes]
+        return WO.at[far, slot, 32 * h:32 * h + 32, lanes]
+
     wb = Two(cop, block, y, ydev, wb_s, wb_r)
+    wf = Two(cop, far_block, y, ydev, wy_s, wy_r)
     wz = {}
     wcs = []
 
@@ -269,15 +283,8 @@
                     wz_s.at[way, 0, n], wz_r.at[way, 0, n], xdev(step),
                 )
 
-    def along_x_again(*ns):
-        for n in ns:
-            slot = wrap(y + n, NY)
-            for way, step in ((0, 1), (1, -1)):
-                wz[way, 0, n].wait_recv()
-                ref = WO.at[wrap(x - step, NX), slot, 32 * way:32 * way + 32, lanes]
-                wz[way, 1, n] = cop.send(ref, ref, wz_s.at[way, 1, n], wz_r.at[way, 1, n], xdev(step))
-
     along_x(0)
+    across = cop.send(wo.at[:, lanes], WO.at[x, y, :, lanes], wz_s.at[0, 1, 0], wz_r.at[0, 1, 0], xdev(2))
 
     quarter = [pl.ds(pl.multiple_of(j * 1024 + h * 512, 512), 512) for h in (0, 1)]
     fx = {}
@@ -423,6 +430,8 @@
     wb.wait(1)
     along_x(1, 7, 2, 6)
     kvring.wait(3, 4)
+    across.wait_recv()
+    wf.start()
     ocp = []
     final = pair(3) + [wrap(y + 4, NY)]
     for d in (3, 2, 1):
@@ -444,7 +453,7 @@
     wb.wait(3, 4)
     along_x(3, 5, 4)
     to_sibling(x)
-    along_x_again(0, 1, 7, 2, 6)
+    wf.forward()
     for cp in ocp:
         cp.wait_recv()
     tops = [jnp.where(x >= d, SB[d, 0:1, :], NEG) for d in range(1, NX)]
@@ -463,14 +472,17 @@
     PK[...] = nt(disp, attended).astype(BF).reshape(NZ, ACAP, HEAD)
     acps = [cop.send(PK.at[wrap(z + k, NZ)], ER.at[z], a_s.at[k], a_r.at[k], zdev(k)) for k in range(1, NZ)]
     ER[z] = PK[z]
-    along_x_again(3, 5, 4)
+    wf.wait(1, 3, 4)
+    to_sibling(far)
+    for cp in wz.values():
+        cp.wait_recv()
     to_sibling(wrap(x - 1, NX), wrap(x + 1, NX))
     forward_weights((0,))
     send_weights((1, 2))
     for cp in acps:
         cp.wait_recv()
     lhs = jnp.concatenate([ER[h] for h in range(NZ)], axis=1)
-    order = [x, wrap(x - 1, NX), wrap(x + 1, NX), wrap(x + 2, NX)]
+    order = [x, far, wrap(x - 1, NX), wrap(x + 1, NX)]
     real = [part(512, b) for b in order]
     ends = {}
 
@@ -497,10 +509,6 @@
     tables = [nn(sel, MG[i]).astype(BF) for i in range(4)]
     picked = [nn(sel, RB[:, real[n]]) for n in range(4)]
     pring.forward(*A)
-    for way in (0, 1):
-        for n in range(NY):
-            wz[way, 1, n].wait_recv()
-    to_sibling(wrap(x + 2, NX))
     project(3)
     pring.forward(*B)
 
@@ -547,7 +555,7 @@
         rows = projected(n)
         h = 2 * (n % 2)
         RES[:, real[n]] = RB[:, real[n]].astype(F32) + nn(MG[h], rows) + nn(MG[h + 1], rows)
-    far_to_sibling((0,))
+    far_to_sibling((0, 1))
     xring.wait(*A, *B)
     for slot in pair(1) + pair(2) + pair(3) + [wrap(y + 4, NY)]:
         normalise(slot)
@@ -555,10 +563,7 @@
     for cp in fcs:
         cp.wait_recv()
     fcs.clear()
-    far_to_sibling((1, 2))
-    for cp in fcs:
-        cp.wait_recv()
-    fcs.clear()
+    far_to_sibling((2,))
     rows = XR[...].reshape(NY * FCAP, D)
     hidden = []
     for n in (0, 256, 512):
@@ -567,6 +572,8 @@
         u = nt(rows, W[1].reshape(704, D)[n:n + size])
         hidden.append((g / (1.0 + jnp.exp(-g)) * u).astype(BF))
     hidden = jnp.concatenate(hidden, axis=1)
+    for cp in fcs:
+        cp.wait_recv()
 
     def cut(ref, k, n):
         return ref.at[k, :, n * 512:(n + 1) * 512]
@@ -612,6 +619,9 @@
                 total = total + (RR, RL)[way][near, :, cols].astype(F32)
         EO[z, :, cols] = total.astype(BF)
         ering.start(n)
+    older = [cp for cp in cop.sent if cp not in ering.cps.values()]
+    for cp in older:
+        cp.wait_send()
     ering.forward(*A, *B)
     for n in range(4):
         cols = slice(n * 512, (n + 1) * 512)
@@ -670,6 +680,7 @@
             dma(NX), dma(NX),
             dma(NX, 2), dma(NX, 2),
             dma(2, 4), dma(2, 4),
+            dma(2, 4), dma(2, 4),
             dma(2, 2, 8), dma(2, 2, 8),
             dma(4), dma(4),
             dma(2, 3, 2), dma(2, 3, 2),

time: 116 us -> 112 us (0.966)
  Pallas kernels: 114 us -> 109 us
    pallas_call x1, Pallas kernels: 114 us -> 109 us  [shards(): pl.pallas_call(layer_kernel, name='layer', out_shape=jax.ShapeDtypeStruct...]
where the time goes in v3:
time: 112 us; the launch traced here: 111 us
  Pallas kernels  109 us (97%)
  local copies, waits for them, and re-layouts  1.88 us (2%)
    pallas_call x1, Pallas kernels, shards(): pl.pallas_call(layer_kernel, name='layer', out_shape=jax.ShapeDtypeStruct...  109 us

profile of v3, /device:TPU:6, one launch (start us, length us, event | category | flops | bytes accessed | tf_op | source)
XLA Modules:
  0.0 110.8 jit_solution(15525642070281522198)
XLA Ops:
  0.0 109.0 %layer.1 = bf16[128,2048]{1,0:T(8,128)(2,1)} custom-call(bf16[128,2048]{1,0:T(8,128)(2,1)} %bitcast.32, bf16[256,128]{1,0:T(8,128)(2,1)} %bitcast.34, bf16[128,128]{1,0:T(8,128)(2,1)} %bitcast.35, bf16[128,128]{1,0:T(8,128)(2,1)} %bitcast.36, s32[2,128]{1,0:T(2,128)} %bitcast.38, f32[2,128]{1,0:T(2,128)} %bitcast.39, s32[2,128]{1,0:T(2,128)} %bitcast.40, ...), custom_call_target="tpu_custom_call" | custom-call | tf_op jit(solution)/shard_map/layer/pallas_call | solution.py:644
  109.0 1.9 %copy.15 = bf16[1,128,2048]{2,1,0:T(8,128)(2,1)} copy(bf16[1,128,2048]{2,1,0:T(8,128)(2,1)} %bitcast.28) | data formatting | bytes 1048576

commit v4 on v3

--- a/solution.py
+++ b/solution.py
@@ -124,21 +124,21 @@
 
 
 class Two:
-    def __init__(self, copies, at, pos, dev, ssem, rsem):
+    def __init__(self, copies, at, pos, dev, ssem, rsem, own=None):
         self.copies, self.at, self.pos, self.dev = copies, at, pos, dev
-        self.ssem, self.rsem = ssem, rsem
+        self.ssem, self.rsem, self.own = ssem, rsem, own
         self.cps = {}
 
-    def _send(self, way, n, ref, k):
+    def _send(self, way, n, ref, k, src=None):
         sign = 1 if way == 0 else -1
         self.cps[way, n] = self.copies.send(
-            ref, ref, self.ssem.at[way, n - 1], self.rsem.at[way, n - 1], self.dev(sign * k)
+            ref if src is None else src, ref, self.ssem.at[way, n - 1], self.rsem.at[way, n - 1], self.dev(sign * k)
         )
 
     def start(self):
         for k in (2, 1):
             for way in (0, 1):
-                self._send(way, k, self.at(self.pos, None), k)
+                self._send(way, k, self.at(self.pos, None), k, self.own)
 
     def forward(self):
         for way in (0, 1):
@@ -241,11 +241,14 @@
     pl.semaphore_wait(barrier, len(partners))
 
     lanes = part(512, j)
-    wait_local(0, 1)
-    kvring = Two(
-        cop, lambda slot, h: KV.at[slot] if h is None else KV.at[slot, h], y, ydev, kv_s, kv_r
-    )
-    kvring.start()
+    def held(i):
+        return lambda slot, h: KV.at[slot, i] if h is None else KV.at[slot, i, 64 * h:64 * h + 64]
+
+    kvrings = [
+        Two(cop, held(i), y, ydev, kv_s.at[i], kv_r.at[i], own) for i, own in enumerate((kk, vv))
+    ]
+    for ring in kvrings:
+        ring.start()
     qcp = {
         d: cop.send(q, QB.at[d], q_s.at[d], q_r.at[d], xdev(-d), sends=x >= d, gets=x + d < NX)
         for d in (3, 2, 1)
@@ -371,7 +374,7 @@
     def pair(step):
         return [wrap(y - step, NY), wrap(y + step, NY)]
 
-    wait_local(2, 9)
+    wait_local(0, 1, 2, 9)
     absorb(0, [y], first=True)
     wb.start()
 
@@ -419,8 +422,10 @@
     mine = iota0(FCAP, TOK) + (z * FCAP).astype(F32)
     sel = ((mine == fslot[:, :TOK]).astype(F32) + (mine == fslot[:, TOK:]).astype(F32)).astype(BF)
 
-    kvring.forward()
-    kvring.wait(1)
+    for ring in kvrings:
+        ring.forward()
+    for ring in kvrings:
+        ring.wait(1)
     near = pair(1) + pair(2)
     absorb(0, near)
     for d in range(1, NX):
@@ -429,7 +434,8 @@
     wb.forward()
     wb.wait(1)
     along_x(1, 7, 2, 6)
-    kvring.wait(3, 4)
+    for ring in kvrings:
+        ring.wait(3, 4)
     across.wait_recv()
     wf.start()
     ocp = []
@@ -676,7 +682,7 @@
             vb(NZ, FCAP, D),
             vf(TOK, D),
             dma(13),
-            dma(2, 4), dma(2, 4),
+            dma(2, 2, 4), dma(2, 2, 4),
             dma(NX), dma(NX),
             dma(NX, 2), dma(NX, 2),
             dma(2, 4), dma(2, 4),

time: 112 us -> 112 us (level)
  no operation moved by 1% of the time
where the time goes in v4:
time: 112 us; the launch traced here: 111 us
  Pallas kernels  110 us (98%)
  local copies, waits for them, and re-layouts  1.88 us (2%)
    pallas_call x1, Pallas kernels, shards(): pl.pallas_call(layer_kernel, name='layer', out_shape=jax.ShapeDtypeStruct...  110 us

profile of v4, /device:TPU:6, one launch (start us, length us, event | category | flops | bytes accessed | tf_op | source)
XLA Modules:
  0.0 111.4 jit_solution(7804887046045066205)
XLA Ops:
  0.0 109.5 %layer.1 = bf16[128,2048]{1,0:T(8,128)(2,1)} custom-call(bf16[128,2048]{1,0:T(8,128)(2,1)} %bitcast.32, bf16[256,128]{1,0:T(8,128)(2,1)} %bitcast.34, bf16[128,128]{1,0:T(8,128)(2,1)} %bitcast.35, bf16[128,128]{1,0:T(8,128)(2,1)} %bitcast.36, s32[2,128]{1,0:T(2,128)} %bitcast.38, f32[2,128]{1,0:T(2,128)} %bitcast.39, s32[2,128]{1,0:T(2,128)} %bitcast.40, ...), custom_call_target="tpu_custom_call" | custom-call | tf_op jit(solution)/shard_map/layer/pallas_call | solution.py:650
  109.5 1.9 %copy.15 = bf16[1,128,2048]{2,1,0:T(8,128)(2,1)} copy(bf16[1,128,2048]{2,1,0:T(8,128)(2,1)} %bitcast.28) | data formatting | bytes 1048576
